TPU v7x, 32 devices: a whole 2x2x4 slice. The times are simulated.
32 devices in a mesh: rep: 2 (over y), seq: 4 (over x, core), fsdp: 4 (over z).
Axes of the slice: x: 2, y: 2, z: 4, core: 2. Of those that a mesh axis runs over, the one named last changes fastest.
Arguments:
- tokens: bfloat16 [16, 1024, 2048], P(('rep', 'fsdp'), 'seq'), may hold values from -6 to 6
- doc_start: int32 [16, 1024], P(('rep', 'fsdp'), 'seq'), may hold values from 0 to 1023, as said below
- cotangent: bfloat16 [16, 1024, 2048], P(('rep', 'fsdp'), 'seq'), may hold values from -6 to 6
- norm_gain: bfloat16 [2048], P(('seq', 'fsdp')), may hold values from 0.5 to 1.5
- input_matrix: bfloat16 [2048, 8512], P(('seq', 'fsdp')), may hold values from -0.125 to 0.125
- conv_weight: bfloat16 [4352, 4], P(('seq', 'fsdp')), may hold values from -3 to 3
- conv_bias: bfloat16 [4352], P(('seq', 'fsdp')), may hold values from -3 to 3
- step_bias: bfloat16 [64], P(('seq', 'fsdp')), may hold values from -6 to -4
- decay_log: bfloat16 [64], P(('seq', 'fsdp')), may hold values from -3.5 to 1.09375
- skip_gain: bfloat16 [64], P(('seq', 'fsdp')), may hold values from 0.5 to 1.5
- gate_gain: bfloat16 [4096], P(('seq', 'fsdp')), may hold values from 0.5 to 1.5
- output_matrix: bfloat16 [4096, 2048], P(('seq', 'fsdp')), may hold values from -0.09375 to 0.09375
Outputs:
- layer_out: bfloat16 [16, 1024, 2048], P(('rep', 'fsdp'), 'seq')
- tokens_grad: float32 [16, 1024, 2048], P(('rep', 'fsdp'), 'seq')
- norm_gain_grad: float32 [2048], P(('seq', 'fsdp'))
- in_projection_grad: float32 [2048, 8512], P(('seq', 'fsdp'))
- conv_weight_grad: float32 [4352, 4], P(('seq', 'fsdp'))
- conv_bias_grad: float32 [4352], P(('seq', 'fsdp'))
- step_bias_grad: float32 [64], P(('seq', 'fsdp'))
- decay_log_grad: float32 [64], P(('seq', 'fsdp'))
- skip_gain_grad: float32 [64], P(('seq', 'fsdp'))
- gate_gain_grad: float32 [4096], P(('seq', 'fsdp'))
- out_projection_grad: float32 [4096, 2048], P(('seq', 'fsdp'))
Inputs may be any that keep to these rules, and one draw needn't show every extreme that they name: `doc_start`: never falls along a sequence; each value is the position, within its sequence, of the first token of that token's document. In each aligned block of 2 sequences one sequence, drawn from the seed, is a single document; every other sequence ends with a document of one token.
All inputs are finite; a program needn't handle non-finite values.
Results may differ from a plain program's by a relative error of at most 0.013.
Values may be sent and summed in bfloat16 or wider, within the bound.
A program may use at most 248 MiB of HBM per device.

v0:
```python
import jax
import jax.numpy as jnp
from jax import lax
from jax.sharding import PartitionSpec as P

DI = 4096
H = 64
PD = 64
N = 128
KW = 4
MICRO = 2


EPSILON = 1e-05
EXACT_MATMUL = lax.Precision.HIGHEST


def passed_along(block, axis, distance):
    devices = range(lax.axis_size(axis))
    route = [(i - distance, i) for i in devices if i - distance in devices]
    return lax.ppermute(block, axis, route)


def prefix(value, axis, join, neutral, backward):
    count, mine = (lax.axis_size(axis), lax.axis_index(axis))
    pieces = jax.tree.map(lambda part: lax.all_gather(part, axis), value)
    if backward:
        pieces = jax.tree.map(lambda part: part[::-1], pieces)
        mine = count - 1 - mine
    subtotal = jax.tree.map(
        lambda part, zero: jnp.full_like(part, 0) + jnp.asarray(zero, part.dtype), value, neutral
    )

    def turn(position, subtotal):
        longer = join(subtotal, jax.tree.map(lambda part: part[position], pieces))
        return jax.tree.map(lambda new, old: jnp.where(position < mine, new, old), longer, subtotal)

    return lax.fori_loop(0, count - 1, turn, subtotal)


def rms_scale(values, gain_vec):
    return (
        values * lax.rsqrt(jnp.mean(values * values, axis=-1, keepdims=True) + EPSILON) * gain_vec
    )


def conv_mix(extended, doc_start, position, conv_weight, conv_bias):
    seq_len = doc_start.shape[1]
    taps = conv_weight.shape[1]
    result = conv_bias
    for offset in range(taps):
        source = position - taps + 1 + offset
        usable = (source[None, :] >= doc_start).astype(jnp.float32)
        result = (
            result
            + conv_weight[:, offset] * extended[:, offset : offset + seq_len] * usable[..., None]
        )
    return result


def local_mix(
    extended,
    step_part,
    doc_start,
    position,
    begin_at,
    conv_weight,
    conv_bias,
    step_bias,
    decay_log,
    skip_gain,
):
    seqs_here, seq_len = doc_start.shape
    activated = jax.nn.silu(conv_mix(extended, doc_start, position, conv_weight, conv_bias))
    head_input = activated[..., :DI].reshape(seqs_here, seq_len, H, PD)
    write_vec = activated[..., DI : DI + N]
    read_vec = activated[..., DI + N :]
    step_size = jax.nn.softplus(step_part + step_bias)
    cum_decay = jnp.cumsum(-jnp.exp(decay_log) * step_size, axis=1)
    same_doc = (
        (doc_start[:, :, None] == doc_start[:, None, :]) & (position[:, None] >= position[None, :])
    )[..., None]
    gaps = cum_decay[:, :, None, :] - cum_decay[:, None, :, :]
    decay_mat = jnp.where(same_doc, jnp.exp(jnp.where(same_doc, gaps, 0.0)), 0.0)
    scores = jnp.einsum(
        "stn,sun->stu",
        read_vec.astype(jnp.bfloat16),
        write_vec.astype(jnp.bfloat16),
        preferred_element_type=jnp.float32,
    )
    mixing = (scores[..., None] * decay_mat * step_size[:, None, :, :]).astype(jnp.bfloat16)
    mixer_out = jnp.einsum(
        "stuh,suhp->sthp",
        mixing,
        head_input.astype(jnp.bfloat16),
        preferred_element_type=jnp.float32,
    )
    mixer_out = (mixer_out + skip_gain[:, None] * head_input).reshape(seqs_here, seq_len, DI)
    final_decay = cum_decay[:, -1:, :]
    last_doc = (doc_start == doc_start[:, -1:])[..., None]
    tail_weight = jnp.exp(final_decay - cum_decay) * last_doc * step_size
    local_state = jnp.einsum(
        "suh,suhp,sun->shpn", tail_weight, head_input, write_vec, precision=EXACT_MATMUL
    )
    through = jnp.exp(final_decay[:, 0]) * (doc_start[:, -1:] < begin_at)
    return (mixer_out, local_state, through, read_vec, cum_decay)


def carried_mix(read_vec, cum_decay, state_in, doc_start, begin_at):
    seqs_here, seq_len = doc_start.shape
    carried = jnp.exp(cum_decay) * (doc_start < begin_at)[..., None]
    mixer_out = (
        jnp.einsum("stn,shpn->sthp", read_vec, state_in, precision=EXACT_MATMUL)
        * carried[..., None]
    )
    return mixer_out.reshape(seqs_here, seq_len, DI)


def chain_link(earlier, later):
    return (earlier[0] * later[0], later[1] + later[0][:, :, None, None] * earlier[1])


def gate_norm(mixer_out, gate_part, gate_scale):
    return rms_scale(mixer_out * jax.nn.silu(gate_part), gate_scale)


def per_device(
    tokens,
    doc_start,
    cotangent,
    norm_gain,
    input_matrix,
    conv_weight,
    conv_bias,
    step_bias,
    decay_log,
    skip_gain,
    gate_gain,
    output_matrix,
):
    shards = (
        norm_gain,
        input_matrix,
        conv_weight,
        conv_bias,
        step_bias,
        decay_log,
        skip_gain,
        gate_gain,
        output_matrix,
    )
    seq_len = tokens.shape[1]
    begin_at = lax.axis_index("seq") * seq_len
    position = begin_at + jnp.arange(seq_len, dtype=jnp.int32)
    rounds_count = MICRO
    per_round = tokens.shape[0] // rounds_count
    channels = DI + 2 * N
    outputs_list = []
    grads_list = []
    owned_sum = None
    for batch_index in range(rounds_count):
        row_low = batch_index * per_round
        row_high = row_low + per_round
        gathered = (
            lax.all_gather(shards[0], ("seq", "fsdp"), axis=0, tiled=True),
            lax.all_gather(shards[1], ("seq", "fsdp"), axis=0, tiled=True),
            lax.all_gather(shards[2], ("seq", "fsdp"), axis=0, tiled=True),
            lax.all_gather(shards[3], ("seq", "fsdp"), axis=0, tiled=True),
            lax.all_gather(shards[4], ("seq", "fsdp"), axis=0, tiled=True),
            lax.all_gather(shards[5], ("seq", "fsdp"), axis=0, tiled=True),
            lax.all_gather(shards[6], ("seq", "fsdp"), axis=0, tiled=True),
            lax.all_gather(shards[7], ("seq", "fsdp"), axis=0, tiled=True),
            lax.all_gather(shards[8], ("seq", "fsdp"), axis=0, tiled=True),
        )
        (
            gain_in,
            projection_input,
            kernel,
            shift_vec,
            bias_step,
            log_rate,
            skip_vec,
            gain_out,
            projection_output,
        ) = gathered
        norm_scale = gain_in.astype(jnp.float32)
        gate_scale = gain_out.astype(jnp.float32)
        small_params = tuple(
            (
                weight_piece.astype(jnp.float32)
                for weight_piece in (kernel, shift_vec, bias_step, log_rate, skip_vec)
            )
        )
        block_tokens = tokens[row_low:row_high]
        block_docs = doc_start[row_low:row_high]
        cotangent_rows = cotangent[row_low:row_high]
        seqs_here = block_tokens.shape[0]
        widened_tokens = block_tokens.astype(jnp.float32)
        normalized_rows, input_pull = jax.vjp(rms_scale, widened_tokens, norm_scale)
        normalized_lowered = normalized_rows.astype(jnp.bfloat16)
        projected_rows = jnp.einsum(
            "oju,uk->ojk", normalized_lowered, projection_input, preferred_element_type=jnp.float32
        ).astype(jnp.bfloat16)
        gate_part = projected_rows[..., :DI].astype(jnp.float32)
        conv_part = projected_rows[..., DI : DI + channels]
        step_part = projected_rows[..., DI + channels :].astype(jnp.float32)
        conv_tail = passed_along(conv_part[:, seq_len - KW + 1 :], "seq", 1)
        extended = jnp.concatenate([conv_tail, conv_part], axis=1).astype(jnp.float32)

        def front_part(extended_in, steps_in, *params):
            return local_mix(extended_in, steps_in, block_docs, position, begin_at, *params)

        front_out, front_pull = jax.vjp(front_part, extended, step_part, *small_params)
        local_out, local_state, through, read_vec, cum_decay = front_out
        identity = (
            jnp.ones((seqs_here, H), jnp.float32),
            jnp.zeros((seqs_here, H, PD, N), jnp.float32),
        )
        state_in = prefix((through, local_state), "seq", chain_link, identity, False)[1]

        def carry_part(read_in, decay_in, state_arg):
            return carried_mix(read_in, decay_in, state_arg, block_docs, begin_at)

        carry_out, carry_pull = jax.vjp(carry_part, read_vec, cum_decay, state_in)
        mixer_out = local_out + carry_out
        mixer_result, gate_pull = jax.vjp(gate_norm, mixer_out, gate_part, gate_scale)
        mixer_lowered = mixer_result.astype(jnp.bfloat16)
        branch_path = jnp.einsum(
            "ucb,by->ucy", mixer_lowered, projection_output, preferred_element_type=jnp.float32
        )
        outputs_list.append((widened_tokens + branch_path).astype(jnp.bfloat16))
        out_grad = jnp.einsum(
            "rpt,rph->th", mixer_lowered, cotangent_rows, preferred_element_type=jnp.float32
        )
        mixed_back = jnp.einsum(
            "tmo,jo->tmj", cotangent_rows, projection_output, preferred_element_type=jnp.float32
        )
        mixer_back, gate_back, gate_grad = gate_pull(mixed_back)
        read_back, cumul_back, state_back = carry_pull(mixer_back)
        adjoint = prefix((through, state_back), "seq", chain_link, identity, True)[1]
        through_back = jnp.sum(adjoint * state_in, axis=(2, 3))
        extended_back, step_back, kernel_grad, shift_grad, bias_grad, rate_grad, skip_grad = (
            front_pull((mixer_back, adjoint, through_back, read_back, cumul_back))
        )
        tail_back = passed_along(extended_back[:, : KW - 1].astype(jnp.bfloat16), "seq", -1).astype(
            jnp.float32
        )
        conv_back = extended_back[:, KW - 1 :] + jnp.pad(
            tail_back, ((0, 0), (seq_len - KW + 1, 0), (0, 0))
        )
        projected_gradient = jnp.concatenate([gate_back, conv_back, step_back], axis=-1).astype(
            jnp.bfloat16
        )
        in_grad = jnp.einsum(
            "vgc,vgi->ci",
            normalized_lowered,
            projected_gradient,
            preferred_element_type=jnp.float32,
        )
        normed_back = jnp.einsum(
            "nzm,hm->nzh", projected_gradient, projection_input, preferred_element_type=jnp.float32
        )
        tokens_back, norm_grad = input_pull(normed_back)
        grads_list.append(cotangent_rows.astype(jnp.float32) + tokens_back)
        terms = (
            norm_grad,
            in_grad,
            kernel_grad,
            shift_grad,
            bias_grad,
            rate_grad,
            skip_grad,
            gate_grad,
            out_grad,
        )
        owned_part = (
            lax.psum_scatter(terms[0], ("seq", "fsdp"), scatter_dimension=0, tiled=True),
            lax.psum_scatter(terms[1], ("seq", "fsdp"), scatter_dimension=0, tiled=True),
            lax.psum_scatter(terms[2], ("seq", "fsdp"), scatter_dimension=0, tiled=True),
            lax.psum_scatter(terms[3], ("seq", "fsdp"), scatter_dimension=0, tiled=True),
            lax.psum_scatter(terms[4], ("seq", "fsdp"), scatter_dimension=0, tiled=True),
            lax.psum_scatter(terms[5], ("seq", "fsdp"), scatter_dimension=0, tiled=True),
            lax.psum_scatter(terms[6], ("seq", "fsdp"), scatter_dimension=0, tiled=True),
            lax.psum_scatter(terms[7], ("seq", "fsdp"), scatter_dimension=0, tiled=True),
            lax.psum_scatter(terms[8], ("seq", "fsdp"), scatter_dimension=0, tiled=True),
        )
        owned_sum = (
            owned_part
            if owned_sum is None
            else tuple(
                (
                    earlier_part + newer_part
                    for earlier_part, newer_part in zip(owned_sum, owned_part)
                )
            )
        )
    summed = lax.psum(owned_sum, "rep")
    return (
        jnp.concatenate(outputs_list, axis=0),
        jnp.concatenate(grads_list, axis=0),
        summed[0],
        summed[1],
        summed[2],
        summed[3],
        summed[4],
        summed[5],
        summed[6],
        summed[7],
        summed[8],
    )


def solution(mesh):
    return jax.shard_map(
        per_device,
        mesh=mesh,
        in_specs=(
            P(("rep", "fsdp"), "seq", None),
            P(("rep", "fsdp"), "seq"),
            P(("rep", "fsdp"), "seq", None),
            P(("seq", "fsdp")),
            P(("seq", "fsdp"), None),
            P(("seq", "fsdp"), None),
            P(("seq", "fsdp")),
            P(("seq", "fsdp")),
            P(("seq", "fsdp")),
            P(("seq", "fsdp")),
            P(("seq", "fsdp")),
            P(("seq", "fsdp"), None),
        ),
        out_specs=(
            P(("rep", "fsdp"), "seq", None),
            P(("rep", "fsdp"), "seq", None),
            P(("seq", "fsdp")),
            P(("seq", "fsdp"), None),
            P(("seq", "fsdp"), None),
            P(("seq", "fsdp")),
            P(("seq", "fsdp")),
            P(("seq", "fsdp")),
            P(("seq", "fsdp")),
            P(("seq", "fsdp")),
            P(("seq", "fsdp"), None),
        ),
        check_vma=False,
    )
```

profile of v0, /device:TPU:0, one launch (start us, length us, event | category | flops | bytes accessed | tf_op | source)
XLA Modules:
  0.0 1879.1 jit_solution(4272122543807423349)
XLA Ops:
  8.7 33.8 %all-gather.5 = bf16[16,1,128]{2,1,0:T(2,128)(2,1)S(1)} all-gather(bf16[1,1,128]{2,1,0:T(2,128)(2,1)} %bitcast.810), channel_id=1, replica_groups=mesh['rep'=2,'seq'=4,'fsdp'=4] {'seq','fsdp'}, dimensions={0}, use_global_device_ids=true | all-gather | bytes 4352 | tf_op jit(solution)/shard_map/all_gather | solution.py:165
  42.6 29.7 %all-gather.4 = bf16[16,272,4]{1,2,0:T(4,128)(2,1)S(1)} all-gather(bf16[1,272,4]{1,2,0:T(4,128)(2,1)} %bitcast.809), channel_id=1, replica_groups=mesh['rep'=2,'seq'=4,'fsdp'=4] {'seq','fsdp'}, dimensions={0}, use_global_device_ids=true | all-gather | bytes 36992 | tf_op jit(solution)/shard_map/all_gather | solution.py:167
  78.6 61.7 %all-reduce.39 = (bf16[4352]{0:T(1024)(128)(2,1)S(1)}, bf16[64]{0:T(256)(128)(2,1)S(1)}, bf16[64]{0:T(256)(128)(2,1)S(1)}, bf16[64]{0:T(256)(128)(2,1)}) all-reduce(bf16[4352]{0:T(1024)(128)(2,1)S(1)} %dynamic-update-slice, bf16[64]{0:T(256)(128)(2,1)S(1)} %dynamic-update-slice.2, ...), channel_id=1, replica_groups=mesh['rep'=2,'seq'=4,'fsdp'=4] {'seq','fsdp'}, use_global_device_ids=true, to_apply=%add.26 | all-reduce | flops 4544 | bytes 18176
  146.2 54.9 %all-gather.14.cloned.1.call-done = bf16[2048,8512]{0,1:T(8,128)(2,1)} async-done(((bf16[128,8512]{0,1:T(8,128)(2,1)}), bf16[2048,8512]{0,1:T(8,128)(2,1)}) %all-gather.14.cloned.1.call-update) | async-done | bytes 34865168 | tf_op jit(solution)/shard_map/all_gather | solution.py:166
  201.1 18.0 fusion.29
  222.2 17.3 fusion.28
  261.6 7.0 fusion.68
  287.7 7.0 fusion.72
  294.8 33.4 %all-gather.6 = bf16[16,1,256]{2,1,0:T(2,128)(2,1)S(1)} all-gather(bf16[1,1,256]{2,1,0:T(2,128)(2,1)S(1)} %reshape.1565), channel_id=1, replica_groups=mesh['rep'=2,'seq'=4,'fsdp'=4] {'seq','fsdp'}, dimensions={0}, use_global_device_ids=true | all-gather | bytes 8704 | tf_op jit(solution)/shard_map/all_gather | solution.py:172
  331.1 13.2 fusion.168
  364.5 9.4 bitcast_add_fusion.4
  380.8 9.3 bitcast_add_fusion.5
  395.8 11.8 while.57
  407.7 8.5 broadcast_multiply_fusion
  428.7 21.2 %all-gather.18.cloned.1.call-done = f32[256,64,128]{2,1,0:T(8,128)} async-done(((f32[64,64,128]{2,1,0:T(8,128)}), f32[256,64,128]{2,1,0:T(8,128)}) %all-gather.18.cloned.1.call-update) | async-done | bytes 8388624 | tf_op jit(solution)/shard_map/all_gather | solution.py:26
  468.6 7.1 multiply_reduce_fusion.13
  475.7 14.8 fusion.57
  490.6 13.1 multiply_reduce_fusion.9
  529.2 11.9 multiply_reduce_fusion.8
  551.3 7.0 fusion.208
  558.5 18.6 fusion.170
  577.1 25.6 %convolution_add_fusion.1 = f32[4096,2048]{1,0:T(8,128)} fusion(f32[4096,2048]{1,0:T(8,128)} %fusion.170, bf16[2,256,2048]{2,1,0:T(8,128)(2,1)} %param.23, f32[1,256,4096]{2,1,0:T(8,128)S(1)} %copy-done.5, f32[256]{0:T(256)S(1)} %fusion.244, f32[4096]{0:T(1024)S(1)} %bitcast.756), kind=kOutput, calls=%fused_computation.39 | convolution fusion | flops 4306501632 | bytes 72369152 | tf_op jit(solution)/shard_map/rpt,rph->th/dot_general | solution.py:232
  614.3 14.7 fusion.25
  635.3 14.6 fusion.27
  667.2 10.4 fusion.150
  684.5 9.8 rev.12
  694.3 11.8 while.58
  706.1 8.3 fusion.64
  714.5 8.3 rev.14
  754.6 10.9 fusion.54
  771.6 10.7 fusion.55
  788.5 9.1 fusion.142
  797.7 9.2 fusion.132
  807.0 7.8 multiply_reduce_fusion.3
  821.8 11.9 multiply_multiply_fusion.3
  833.8 7.9 pad_add_fusion
  843.1 8.7 pad_add_fusion.1
  863.0 27.2 %fusion.117 = f32[2048,8512]{0,1:T(8,128)} fusion(bf16[256,64]{1,0:T(8,128)(2,1)S(1)} %bitcast.763, bf16[256,4352]{1,0:T(8,128)(2,1)} %fusion.80, bf16[256,4096]{1,0:T(8,128)(2,1)} %get-tuple-element.682, f32[2048]{0:T(1024)S(1)} %bitcast.748, f32[256]{0:T(256)S(1)} %copy-done.42, bf16[2,256,2048]{2,1,0:T(8,128)(2,1)S(1)} %copy-done.13), kind=kOutput, calls=%fused_computation.217 | convolution fusion | flops 8940650496 | bytes 75179008 | tf_op jit(solution)/shard_map/vgc,vgi->ci/dot_general | solution.py:254
  890.2 48.0 %convolution_add_fusion = f32[2048,8512]{0,1:T(8,128)} fusion(f32[2048,8512]{0,1:T(8,128)} %fusion.117, bf16[256,64]{1,0:T(8,128)(2,1)S(1)} %bitcast.765, bf16[256,4352]{1,0:T(8,128)(2,1)} %fusion.81, bf16[256,4096]{1,0:T(8,128)(2,1)} %get-tuple-element.683, f32[256]{0:T(256)S(1)} %copy-done.40, f32[2048]{0:T(1024)S(1)} %bitcast.749, ...), kind=kOutput, calls=%fused_computation.12 | convolution fusion | flops 8958083072 | bytes 144909312 | tf_op jit(solution)/shard_map/vgc,vgi->ci/dot_general | solution.py:254
  941.2 12.1 fusion.75
  953.3 8.6 fusion.74
  965.8 10.5 reduce-scatter.8.cloned.1.call-done
  976.3 665.3 %reduce-scatter.6.cloned.1.call-done = f32[128,8512]{0,1:T(8,128)} async-done(((f32[2048,8512]{0,1:T(8,128)}), f32[128,8512]{0,1:T(8,128)}) %reduce-scatter.6.cloned.1.call-update) | async-done | bytes 4358160 | tf_op jit(solution)/shard_map/reduce_scatter | solution.py:278
  1641.7 18.5 fusion.116
  1660.2 19.1 %fusion.85 = (f32[2048]{0:T(1024)S(1)}, f32[256]{0:T(256)S(1)}, f32[256]{0:T(256)S(1)}, f32[2048]{0:T(1024)S(1)}, f32[256,2048]{1,0:T(8,128)}) fusion(f32[256]{0:T(256)S(1)} %copy-done.42, bf16[2,256,2048]{2,1,0:T(8,128)(2,1)S(1)} %copy-done.13, f32[2048]{0:T(1024)S(1)} %bitcast.750, f32[256,2048]{1,0:T(8,128)} %fusion.116, f32[256]{0:T(256)S(1)} %copy-done.40, ...), kind=kOutput, calls=%fused_computation.180 | convolution fusion | flops 8945889280 | bytes 45543424 | tf_op jit(solution)/shard_map/nzm,hm->nzh/dot_general | solution.py:260
  1679.3 60.5 %all-reduce.36 = (f32[2048]{0:T(1024)S(1)}, f32[4352]{0:T(1024)S(1)}, f32[64]{0:T(128)S(1)}, f32[64]{0:T(128)S(1)}, f32[64]{0:T(128)S(1)}, /*index=5*/f32[4096]{0:T(1024)S(1)}) all-reduce(f32[2048]{0:T(1024)S(1)} %add.557, f32[4352]{0:T(1024)S(1)} %add.560, ...), channel_id=15, replica_groups=mesh['rep'=2,'seq'=4,'fsdp'=4] {'seq','fsdp'}, use_global_device_ids=true, to_apply=%region_39.41.clone | all-reduce | flops 10688 | bytes 85504
  1747.0 9.0 all-reduce.37
  1756.0 110.5 %all-reduce.42.cloned.1.call-done = (f32[128,8512]{0,1:T(8,128)}, f32[256,2048]{1,0:T(8,128)}) async-done(((f32[128,8512]{0,1:T(8,128)}, f32[256,2048]{1,0:T(8,128)}), (f32[128,8512]{0,1:T(8,128)}, f32[256,2048]{1,0:T(8,128)})) %all-reduce.42.cloned.1.call-update) | async-done | bytes 6455312 | tf_op jit(solution)/shard_map/psum | solution.py:297
  (509 shorter events, 315.2 us)
Async XLA Ops:
  7.2 137.1 %copy-start.101 = (s32[2,256]{1,0:T(2,128)S(1)}, s32[2,256]{1,0:T(2,128)}, u32[]{:S(2)}) copy-start(s32[2,256]{1,0:T(2,128)} %param.22) | copy-start | bytes 6148
  7.2 136.0 %copy-start.12 = (bf16[2,256,2048]{2,1,0:T(8,128)(2,1)S(1)}, bf16[2,256,2048]{2,1,0:T(8,128)(2,1)}, u32[]{:S(2)}) copy-start(bf16[2,256,2048]{2,1,0:T(8,128)(2,1)} %param.21) | copy-start | bytes 6291460
  7.2 193.9 %all-gather.14.cloned.1.call-start = ((), (), s32[]{:S(2)}) async-start(), calls=%async_computation.3 | async-start | bytes 37044224 | tf_op jit(solution)/shard_map/all_gather | solution.py:166
  7.9 323.2 %all-gather.16.cloned.1.call-start = ((), (), s32[]{:S(2)}) async-start(), calls=%async_computation.4 | async-start | bytes 17825792 | tf_op jit(solution)/shard_map/all_gather | solution.py:173
  8.7 387.1 %all-gather.20.cloned.1.call-start = ((), (), s32[]{:S(2)}) async-start(), calls=%async_computation.6 | async-start | bytes 10485760 | tf_op jit(solution)/shard_map/all_gather | solution.py:26
  42.6 179.5 %copy-start.25 = (f32[16,1,128]{2,1,0:T(1,128)}, f32[16,1,128]{2,1,0:T(1,128)S(1)}, u32[]{:S(2)}) copy-start(f32[16,1,128]{2,1,0:T(1,128)S(1)} %convert_element_type.391) | copy-start | bytes 24580
  140.2 78.9 %copy-start.123 = (bf16[64]{0:T(256)(128)(2,1)}, bf16[64]{0:T(256)(128)(2,1)S(1)}, u32[]{:S(2)}) copy-start(bf16[64]{0:T(256)(128)(2,1)S(1)} %get-tuple-element.656) | copy-start | bytes 388
  142.3 97.2 %copy-start.77 = (f32[64]{0:T(128)}, f32[64]{0:T(128)S(1)}, u32[]{:S(2)}) copy-start(f32[64]{0:T(128)S(1)} %convert_element_type.320) | copy-start | bytes 772
  143.1 129.2 %copy-start.43 = (f32[4352]{0:T(1024)}, f32[4352]{0:T(1024)S(1)}, u32[]{:S(2)}) copy-start(f32[4352]{0:T(1024)S(1)} %get-tuple-element.591) | copy-start | bytes 52228
  143.1 129.2 %copy-start.45 = (f32[4352]{0:T(1024)}, f32[4352]{0:T(1024)S(1)}, u32[]{:S(2)}) copy-start(f32[4352]{0:T(1024)S(1)} %get-tuple-element.592) | copy-start | bytes 52228
  143.1 129.2 %copy-start.47 = (f32[4352]{0:T(1024)}, f32[4352]{0:T(1024)S(1)}, u32[]{:S(2)}) copy-start(f32[4352]{0:T(1024)S(1)} %get-tuple-element.593) | copy-start | bytes 52228
  143.1 129.2 %copy-start.49 = (f32[4352]{0:T(1024)}, f32[4352]{0:T(1024)S(1)}, u32[]{:S(2)}) copy-start(f32[4352]{0:T(1024)S(1)} %get-tuple-element.594) | copy-start | bytes 52228
  143.2 96.3 %copy-start.119 = (f32[64]{0:T(128)}, f32[64]{0:T(128)S(1)}, u32[]{:S(2)}) copy-start(f32[64]{0:T(128)S(1)} %fusion.245) | copy-start | bytes 772
  143.7 75.4 %copy-start.109 = (f32[256]{0:T(256)}, f32[256]{0:T(256)S(1)}, u32[]{:S(2)}) copy-start(f32[256]{0:T(256)S(1)} %get-tuple-element.589) | copy-start | bytes 3076
  144.3 74.9 %copy-start.39 = (f32[256]{0:T(256)}, f32[256]{0:T(256)S(1)}, u32[]{:S(2)}) copy-start(f32[256]{0:T(256)S(1)} %fusion.243) | copy-start | bytes 3076
  144.3 77.9 %copy-start.41 = (f32[256]{0:T(256)}, f32[256]{0:T(256)S(1)}, u32[]{:S(2)}) copy-start(f32[256]{0:T(256)S(1)} %fusion.241) | copy-start | bytes 3076
  146.2 96.5 %copy-start.115 = (f32[1,256]{1,0:T(1,128)}, f32[1,256]{1,0:T(1,128)S(1)}, u32[]{:S(2)}) copy-start(f32[1,256]{1,0:T(1,128)S(1)} %get-tuple-element.715) | copy-start | bytes 3076
  146.2 96.7 %copy-start.113 = (f32[1,256]{1,0:T(1,128)}, f32[1,256]{1,0:T(1,128)S(1)}, u32[]{:S(2)}) copy-start(f32[1,256]{1,0:T(1,128)S(1)} %get-tuple-element.721) | copy-start | bytes 3076
  146.2 97.9 %copy-start.73 = (f32[1,256]{1,0:T(1,128)}, f32[1,256]{1,0:T(1,128)S(1)}, u32[]{:S(2)}) copy-start(f32[1,256]{1,0:T(1,128)S(1)} %get-tuple-element.720) | copy-start | bytes 3076
  146.2 97.9 %copy-start.75 = (f32[1,256]{1,0:T(1,128)}, f32[1,256]{1,0:T(1,128)S(1)}, u32[]{:S(2)}) copy-start(f32[1,256]{1,0:T(1,128)S(1)} %get-tuple-element.710) | copy-start | bytes 3076
  220.6 24.7 %collective-permute-start.1 = (bf16[1,3,4352]{2,1,0:T(4,128)(2,1)}, bf16[1,3,4352]{2,1,0:T(4,128)(2,1)S(1)}, u32[]{:S(2)}, u32[]{:S(2)}) collective-permute-start(bf16[1,3,4352]{2,1,0:T(4,128)(2,1)} %slice.221), channel_id=1, source_target_pairs={{0,4},{4,8},{8,12},{1,5},{5,9},{9,13},{2,6},{6,10},{10,14},{3,7},{... | collective-permute-start | bytes 78344 | tf_op jit(solution)/shard_map/ppermute | solution.py:21
  242.8 101.9 %copy-start.21 = (f32[1,64,256]{1,2,0:T(8,128)}, f32[1,64,256]{1,2,0:T(8,128)S(1)}, u32[]{:S(2)}) copy-start(f32[1,64,256]{1,2,0:T(8,128)S(1)} %get-tuple-element.672) | copy-start | bytes 196612
  243.0 101.4 %copy-start.23 = (f32[1,64,256]{1,2,0:T(8,128)}, f32[1,64,256]{1,2,0:T(8,128)S(1)}, u32[]{:S(2)}) copy-start(f32[1,64,256]{1,2,0:T(8,128)S(1)} %get-tuple-element.679) | copy-start | bytes 196612
  268.6 181.3 %all-gather.18.cloned.1.call-start = ((), (), s32[]{:S(2)}) async-start(), calls=%async_computation.5 | async-start | bytes 10485760 | tf_op jit(solution)/shard_map/all_gather | solution.py:26
  269.7 2.1 collective-permute-start
  287.7 40.6 %copy-start.102 = (s32[2,256]{1,0:T(2,128)S(1)}, s32[2,256]{1,0:T(2,128)}, u32[]{:S(2)}) copy-start(s32[2,256]{1,0:T(2,128)} %param.22) | copy-start | bytes 6148
  294.7 389.8 %all-gather.22.cloned.1.call-start = ((), (), s32[]{:S(2)}) async-start(), calls=%async_computation.7 | async-start | bytes 10485760 | tf_op jit(solution)/shard_map/all_gather | solution.py:26
  294.8 86.0 %copy-start.127 = (f32[64]{0:T(128)}, f32[64]{0:T(128)S(1)}, u32[]{:S(2)}) copy-start(f32[64]{0:T(128)S(1)} %convert_element_type.322) | copy-start | bytes 772
  328.2 248.8 %copy-start.28 = (f32[16,1,256]{2,1,0:T(1,128)}, f32[16,1,256]{2,1,0:T(1,128)S(1)}, u32[]{:S(2)}) copy-start(f32[16,1,256]{2,1,0:T(1,128)S(1)} %convert_element_type.392) | copy-start | bytes 49156
  328.5 36.0 %copy-start.67 = (pred[256,256]{1,0:T(8,128)(4,1)}, pred[256,256]{1,0:T(8,128)(4,1)S(1)}, u32[]{:S(2)}) copy-start(pred[256,256]{1,0:T(8,128)(4,1)S(1)} %get-tuple-element.727) | copy-start | bytes 196612
  328.5 285.8 %copy-start.66 = (pred[256,256]{1,0:T(8,128)(4,1)}, pred[256,256]{1,0:T(8,128)(4,1)S(1)}, u32[]{:S(2)}) copy-start(pred[256,256]{1,0:T(8,128)(4,1)S(1)} %get-tuple-element.726) | copy-start | bytes 196612
  344.4 20.1 %copy-start.62 = (f32[256,64]{0,1:T(8,128)}, f32[256,64]{0,1:T(8,128)S(1)}, u32[]{:S(2)}) copy-start(f32[256,64]{0,1:T(8,128)S(1)} %copy.338) | copy-start | bytes 196612
  344.7 269.6 %copy-start.58 = (f32[256,64]{0,1:T(8,128)}, f32[256,64]{0,1:T(8,128)S(1)}, u32[]{:S(2)}) copy-start(f32[256,64]{0,1:T(8,128)S(1)} %copy.325) | copy-start | bytes 196612
  344.8 269.5 %copy-start.60 = (f32[256,64]{0,1:T(8,128)}, f32[256,64]{0,1:T(8,128)S(1)}, u32[]{:S(2)}) copy-start(f32[256,64]{0,1:T(8,128)S(1)} %copy.323) | copy-start | bytes 196612
  380.8 233.5 %copy-start.51 = (f32[256,256]{1,0:T(8,128)}, f32[256,256]{1,0:T(8,128)S(1)}, u32[]{:S(2)}) copy-start(f32[256,256]{1,0:T(8,128)S(1)} %fusion.234) | copy-start | bytes 786436
  428.7 148.4 %copy-start.69 = (f32[256]{0:T(256)}, f32[256]{0:T(256)S(1)}, u32[]{:S(2)}) copy-start(f32[256]{0:T(256)S(1)} %fusion.244) | copy-start | bytes 3076
  475.7 82.8 %copy-start.71 = (f32[256]{0:T(256)}, f32[256]{0:T(256)S(1)}, u32[]{:S(2)}) copy-start(f32[256]{0:T(256)S(1)} %fusion.242) | copy-start | bytes 3076
  521.1 193.4 %all-gather.24.cloned.1.call-start = ((), (), s32[]{:S(2)}) async-start(), calls=%async_computation.8 | async-start | bytes 10485760 | tf_op jit(solution)/shard_map/all_gather | solution.py:26
  558.3 418.0 %reduce-scatter.8.cloned.1.call-start = ((), (), s32[]{:S(2)}) async-start(), calls=%async_computation.10 | async-start | bytes 35651584 | tf_op jit(solution)/shard_map/reduce_scatter | solution.py:285
  602.8 1038.9 %reduce-scatter.6.cloned.1.call-start = ((), (), s32[]{:S(2)}) async-start(), calls=%async_computation.9 | async-start | bytes 74088448 | tf_op jit(solution)/shard_map/reduce_scatter | solution.py:278
  782.3 24.5 %slice-start = ((s8[4595712]{0:T(1024)(128)(4,1)}), s8[401408]{0:T(1024)(128)(4,1)S(1)}, s32[]{:S(2)}) async-start(s8[4595712]{0:T(1024)(128)(4,1)} %bitcast.698), calls=%async_computation.13 | async-start | bytes 802816
  841.7 15.1 collective-permute-start.3
  853.1 7.8 collective-permute-start.2
  863.0 27.2 %copy-start.40 = (f32[256]{0:T(256)S(1)}, f32[256]{0:T(256)}, u32[]{:S(2)}) copy-start(f32[256]{0:T(256)} %copy-done.39) | copy-start | bytes 3076
  938.2 807.8 %reduce-scatter.10.cloned.1.call-start = ((), (), s32[]{:S(2)}) async-start(), calls=%async_computation.11 | async-start | bytes 2367488
  965.7 900.8 %all-reduce.42.cloned.1.call-start = ((), (), s32[]{:S(2)}) async-start(), calls=%async_computation.12 | async-start | bytes 12910592 | tf_op jit(solution)/shard_map/psum | solution.py:297
  1660.2 80.0 %copy-start.110 = (f32[256]{0:T(256)S(1)}, f32[256]{0:T(256)}, u32[]{:S(2)}) copy-start(f32[256]{0:T(256)} %copy-done.109) | copy-start | bytes 3076
  1660.2 80.0 %copy-start.112 = (f32[256]{0:T(256)S(1)}, f32[256]{0:T(256)}, u32[]{:S(2)}) copy-start(f32[256]{0:T(256)} %copy-done.111) | copy-start | bytes 3076
  (103 other events, 834.9 us)
Sparse Core Ops, SparseCore 0:
  9.5 191.5 all-gather.13
  203.3 127.7 all-gather.15
  333.2 56.8 all-gather.19
  391.5 58.2 all-gather.17
  521.3 58.2 all-gather.21
  581.0 58.2 all-gather.23
  643.6 332.7 reduce-scatter.7
  980.6 661.0 reduce-scatter.5
  1645.9 61.6 reduce-scatter.9
  1710.0 156.5 all-reduce.41
where the time goes:
time: 1890 us; the launch traced here: 1880 us
  waiting for transfers between devices  867 us (46%)
  matrix products  414 us (22%)
  blocking collectives  239 us (13%)
  other arithmetic  184 us (10%)
  local copies, waits for them, and re-layouts  146 us (8%)
  between operations  22 us (1%)
    reduce_scatter x1, waiting for transfers between devices, per_device(): lax.psum_scatter(terms[1], ('seq', 'fsdp'), scatter_dimension=0, tiled=True)  665 us
    unnamed x2, blocking collectives  122 us
    psum x1, waiting for transfers between devices, per_device(): summed = lax.psum(owned_sum, 'rep')  111 us
    dot_general x2, matrix products, per_device(): jnp.einsum('vgc,vgi->ci', normalized_lowered, projected_gradient, preferr...  75.2 us
    dot_general x6, matrix products, local_mix(): jnp.einsum('stuh,suhp->sthp', mixing, head_input.astype(jnp.bfloat16), pr...  69.8 us
    all_gather x1, waiting for transfers between devices, per_device(): lax.all_gather(shards[1], ('seq', 'fsdp'), axis=0, tiled=True)  54.9 us
    dot_general x6, matrix products, local_mix(): jnp.einsum('suh,suhp,sun->shpn', tail_weight, head_input, write_vec, prec...  47.2 us
    dot_general x6, matrix products, carried_mix(): jnp.einsum('stn,shpn->sthp', read_vec, state_in, precision=EXACT_MATMUL)  46.4 us
  transfers between devices with their start and end apart: 14, of which 7 were waited for; matrix products, arithmetic and copies ran while one was open for 35% of the time, Pallas kernels for 0%

commit v1 on v0

v1 whole, which is shorter than its diff:
```python
import functools

import jax
import jax.numpy as jnp
import numpy as np
from jax import lax
from jax.experimental import pallas as pl
from jax.experimental.pallas import tpu as pltpu
from jax.sharding import Mesh, PartitionSpec as P

DI = 4096
H = 64
PD = 64
N = 128
KW = 4
EPSILON = 1e-05
LANES = 128
BF = jnp.bfloat16
F32 = jnp.float32
FAR = -1e30


def dot(a, b, dims):
    return lax.dot_general(a, b, (dims, ((), ())), preferred_element_type=F32)


def nn(a, b):
    return dot(a, b, ((1,), (0,)))


def nt(a, b):
    return dot(a, b, ((1,), (1,)))


def tn(a, b):
    return dot(a, b, ((0,), (0,)))


def split_rows(v, parts):
    pieces = []
    for _ in range(parts):
        high = v.astype(BF).astype(F32)
        pieces.append(high)
        v = v - high
    return jnp.concatenate(pieces, axis=0).astype(BF)


def running_sum(v, triangle):
    rows = v.shape[0]
    total = nn(split_rows(v, 3), triangle)
    return total[:rows] + total[rows : 2 * rows] + total[2 * rows :]


def softplus(v):
    e = jnp.exp(-jnp.abs(v))
    return jnp.maximum(v, 0.0) + jnp.log1p(e)


def sigmoid(v):
    return 1.0 / (1.0 + jnp.exp(-v))


def column_of_row(row, width):
    high = row.astype(BF).astype(F32)
    rows = lax.broadcasted_iota(jnp.int32, (8, row.shape[1]), 0)
    stack = jnp.where(rows == 0, high, jnp.where(rows == 1, row - high, 0.0)).astype(BF)
    return tn(stack, jnp.ones((8, width), BF))


def scan_front(s, span, x_ref, xt_ref, bc_ref, bct_ref, st_ref, doc_ref, cw_ref, hp_ref, e3_ref, i3_ref, tri_ref, ext):
    ch = x_ref.shape[-1]
    wide = ext.shape[1]
    zero_tail = s == 0
    xt = xt_ref[...].astype(F32)
    bct = bct_ref[...].astype(F32)
    ext[0:16, :ch] = jnp.where(zero_tail, 0.0, xt)
    ext[0:16, ch:] = jnp.where(zero_tail, 0.0, bct)
    ext[16:, :ch] = x_ref[...].astype(F32)
    ext[16:, ch:] = bc_ref[...].astype(F32)
    doc_row = doc_ref[...]
    doc_col = column_of_row(doc_row, LANES)
    begin = s * span
    at = (begin + lax.broadcasted_iota(jnp.int32, (span, LANES), 0)).astype(F32)
    since = at - doc_col
    usable = [(since >= float(KW - 1 - k)).astype(F32) for k in range(KW - 1)]

    def pre_of(c):
        cols = slice(c * LANES, (c + 1) * LANES)
        shifted = [ext[16 - KW + 1 + k : 16 - KW + 1 + k + span, cols] for k in range(KW)]
        masked = [shifted[k] * usable[k] for k in range(KW - 1)] + [shifted[KW - 1]]
        pre = cw_ref[KW : KW + 1, cols]
        for k in range(KW):
            pre = pre + cw_ref[k : k + 1, cols] * masked[k]
        return pre, masked

    heads = hp_ref.shape[0]
    raw = jnp.transpose(st_ref[...].astype(F32))[:heads]
    raw = raw + hp_ref[:, 0:1]
    step = softplus(raw)
    rate = -jnp.exp(hp_ref[:, 1:2])
    log_decay = rate * step
    cum = running_sum(log_decay, tri_ref[...])
    cum_col = tn(split_rows(cum, 3), i3_ref[...])
    last = cum[:, span - 1 : span]
    doc8 = jnp.broadcast_to(doc_row, (heads, span))
    begin_f = begin.astype(F32)
    carried = jnp.where(doc8 < begin_f, jnp.exp(cum), 0.0)
    tail = jnp.where(doc8 == doc_row[:, span - 1 : span], jnp.exp(last - cum), 0.0)
    e3 = e3_ref[...]
    step_x = tn(split_rows(step, 3), e3)
    carried_x = tn(split_rows(carried, 3), e3)
    tail_x = tn(split_rows(tail, 3), e3)
    return dict(
        doc_row=doc_row, doc_col=doc_col, usable=usable, pre_of=pre_of, raw=raw, step=step, rate=rate,
        log_decay=log_decay, cum=cum, cum_col=cum_col, step_x=step_x, carried_x=carried_x, tail_x=tail_x, begin_f=begin_f,
    )


def forward_kernel(x_ref, xt_ref, bc_ref, bct_ref, g_ref, st_ref, doc_ref, cw_ref, hp_ref, sk_ref, e3_ref, i3_ref, tri_ref,
                   y_ref, gated_ref, s1_ref, entry_ref, ext, act, state):
    s = pl.program_id(1)
    span, ch = x_ref.shape
    wide = ext.shape[1]

    @pl.when(s == 0)
    def _():
        state[...] = jnp.zeros_like(state)

    f = scan_front(s, span, x_ref, xt_ref, bc_ref, bct_ref, st_ref, doc_ref, cw_ref, hp_ref, e3_ref, i3_ref, tri_ref, ext)
    for c in range(wide // LANES):
        pre, _ = f["pre_of"](c)
        act[:, c * LANES : (c + 1) * LANES] = pre * sigmoid(pre)
    entry_ref[...] = state[...]
    write = act[:, ch : ch + N].astype(BF)
    read = act[:, ch + N :].astype(BF)
    scores = nt(read, write)
    row = lax.broadcasted_iota(jnp.int32, (span, span), 0)
    col = lax.broadcasted_iota(jnp.int32, (span, span), 1)
    doc_wide = jnp.concatenate([f["doc_col"]] * (span // LANES), axis=1)
    inside = (col.astype(F32) + f["begin_f"] >= doc_wide) & (col <= row)
    bias = jnp.where(inside, 0.0, FAR)
    lane = lax.broadcasted_iota(jnp.int32, (span, LANES), 1)
    per = LANES // PD
    squares = jnp.zeros((span, LANES), F32)
    for j in range(ch // LANES):
        cols = slice(j * LANES, (j + 1) * LANES)
        x = act[:, cols]
        xd = (x * f["step_x"][:, cols]).astype(BF)
        y = jnp.zeros((span, LANES), F32)
        for i in range(per):
            h = j * per + i
            gap = f["cum_col"][:, h : h + 1] - f["cum"][h : h + 1, :] + bias
            mixing = (scores * jnp.exp(gap)).astype(BF)
            y = jnp.where((lane >= i * PD) & (lane < (i + 1) * PD), nn(mixing, xd), y)
        before = state[:, cols]
        y = y + f["carried_x"][:, cols] * nn(read, before.astype(BF))
        y = y + sk_ref[:, cols] * x
        through = f["carried_x"][span - 1 : span, cols]
        built = tn(write, (xd.astype(F32) * f["tail_x"][:, cols]).astype(BF))
        state[:, cols] = through * before + built
        g = g_ref[:, cols].astype(F32)
        gated = y * g * sigmoid(g)
        y_ref[:, cols] = y.astype(BF)
        gated_ref[:, cols] = gated.astype(BF)
        squares = squares + gated * gated
    s1_ref[...] = nt(jnp.ones((8, LANES), BF), squares.astype(BF))


def backward_kernel(x_ref, xt_ref, bc_ref, bct_ref, g_ref, st_ref, doc_ref, cw_ref, hp_ref, sk_ref, e3_ref, i3_ref, tri_ref,
                    low_ref, pick_ref, y_ref, t1_ref, stat_ref, entry_ref,
                    pb_ref, cg_ref, hg_ref, sg_ref,
                    ext, act, dfac, shifted_back, adj, score_back, rows8):
    step_id = pl.program_id(1)
    s = pl.num_programs(1) - 1 - step_id
    span, ch = x_ref.shape
    wide = ext.shape[1]
    heads = hp_ref.shape[0]

    @pl.when(step_id == 0)
    def _():
        adj[...] = jnp.zeros_like(adj)
        shifted_back[...] = jnp.zeros_like(shifted_back)

    @pl.when((step_id == 0) & (pl.program_id(0) == 0))
    def _():
        cg_ref[...] = jnp.zeros_like(cg_ref)
        hg_ref[...] = jnp.zeros_like(hg_ref)
        sg_ref[...] = jnp.zeros_like(sg_ref)

    f = scan_front(s, span, x_ref, xt_ref, bc_ref, bct_ref, st_ref, doc_ref, cw_ref, hp_ref, e3_ref, i3_ref, tri_ref, ext)
    for c in range(wide // LANES):
        cols = slice(c * LANES, (c + 1) * LANES)
        pre, _ = f["pre_of"](c)
        sg = sigmoid(pre)
        act[:, cols] = pre * sg
        dfac[:, cols] = sg * (1.0 + pre * (1.0 - sg))
    write = act[:, ch : ch + N].astype(BF)
    read = act[:, ch + N :].astype(BF)
    scores_t = nt(write, read)
    row = lax.broadcasted_iota(jnp.int32, (span, span), 0)
    col = lax.broadcasted_iota(jnp.int32, (span, span), 1)
    inside = (row.astype(F32) + f["begin_f"] >= f["doc_row"]) & (row <= col)
    bias = jnp.where(inside, 0.0, FAR)
    lane = lax.broadcasted_iota(jnp.int32, (span, LANES), 1)
    lane1 = lax.broadcasted_iota(jnp.int32, (1, LANES), 1)
    last1 = lax.broadcasted_iota(jnp.int32, (1, span), 1) == span - 1
    per = LANES // PD
    stat = tn(split_rows(stat_ref[...], 3), pick_ref[...])
    inv = stat[:, :LANES]
    kk = stat[:, LANES:]
    score_back[...] = jnp.zeros_like(score_back)
    head_rows = jnp.zeros((heads, span), F32)
    size_rows = jnp.zeros((heads, span), F32)
    write_back = jnp.zeros((span, N), F32)
    read_back = jnp.zeros((span, N), F32)
    for j in range(ch // LANES):
        cols = slice(j * LANES, (j + 1) * LANES)
        x = act[:, cols]
        step_x = f["step_x"][:, cols]
        tail_x = f["tail_x"][:, cols]
        carried_x = f["carried_x"][:, cols]
        xd = (x * step_x).astype(BF)
        g = g_ref[:, cols].astype(F32)
        y = y_ref[:, cols].astype(F32)
        sg = sigmoid(g)
        silu = g * sg
        gated_back = inv * t1_ref[:, cols].astype(F32) - kk * (y * silu)
        dy = gated_back * silu
        pb_ref[:, ch + j * LANES : ch + (j + 1) * LANES] = (gated_back * y * (sg * (1.0 + g * (1.0 - sg)))).astype(BF)
        dyb = dy.astype(BF)
        sg_ref[0:1, cols] += jnp.sum(dy * x, axis=0, keepdims=True)
        before = entry_ref[:, cols]
        before_b = before.astype(BF)
        after = adj[:, cols]
        after_b = after.astype(BF)
        through = carried_x[span - 1 : span, :]
        dyc = (dy * carried_x).astype(BF)
        carry_y = carried_x * nn(read, before_b)
        read_back = read_back + nt(dyc, before_b)
        tail_back = tail_x * nn(write, after_b)
        xd_f = xd.astype(F32)
        write_back = write_back + nt((xd_f * tail_x).astype(BF), after_b)
        ends = through * jnp.sum(after * before, axis=0, keepdims=True) + jnp.sum(xd_f * tail_back, axis=0, keepdims=True)
        adj[:, cols] = through * after + tn(read, dyc)
        xd_back = tail_back
        for i in range(per):
            h = j * per + i
            mine = (lane >= i * PD) & (lane < (i + 1) * PD)
            gap = f["cum"][h : h + 1, :] - f["cum_col"][:, h : h + 1] + bias
            decay = jnp.exp(gap)
            mixing = (scores_t * decay).astype(BF)
            mixing_back = nt(jnp.where(mine, xd, jnp.zeros_like(xd)), dyb)
            score_back[...] += mixing_back * decay
            sums = jnp.sum(mixing_back * mixing.astype(F32), axis=0, keepdims=True)
            mine1 = (lane1 >= i * PD) & (lane1 < (i + 1) * PD)
            end = jnp.sum(jnp.where(mine1, ends, 0.0), axis=1, keepdims=True)
            rows8[h : h + 1, :] = sums + jnp.where(last1, end, 0.0)
            xd_back = xd_back + jnp.where(mine, nn(mixing, dyb), 0.0)
        act_back = sk_ref[:, cols] * dy + step_x * xd_back
        part = dy * carry_y - xd_f * xd_back
        high = part.astype(BF)
        low = (part - high.astype(F32)).astype(BF)
        e1 = e3_ref[0:heads, cols]
        head_rows = head_rows + nt(e1, high) + nt(e1, low)
        size_rows = size_rows + nt(e1, (x * xd_back).astype(BF))
        dfac[:, cols] = dfac[:, cols] * act_back
    sb = score_back[...].astype(BF)
    write_back = write_back + nn(sb, read)
    read_back = read_back + tn(sb, write)
    dfac[:, ch : ch + N] = dfac[:, ch : ch + N] * write_back
    dfac[:, ch + N :] = dfac[:, ch + N :] * read_back

    decay_back = running_sum(rows8[0:heads, :] + head_rows, low_ref[...])
    at_row = (s * span).astype(F32) + lax.broadcasted_iota(jnp.int32, (heads, span), 1).astype(F32)
    decay_back = jnp.where(at_row > f["doc_row"], decay_back, 0.0)
    step_back = (size_rows + f["rate"] * decay_back) * sigmoid(f["raw"])
    hg_ref[0:heads, :] += step_back
    hg_ref[heads : 2 * heads, :] += decay_back * f["log_decay"]
    padded = jnp.concatenate([step_back, jnp.zeros((LANES - heads, span), F32)], axis=0)
    pb_ref[:, 2 * ch + 2 * N :] = jnp.transpose(padded).astype(BF)

    for c in range(wide // LANES):
        cols = slice(c * LANES, (c + 1) * LANES)
        _, masked = f["pre_of"](c)
        pre_back = dfac[:, cols]
        for k in range(KW):
            cg_ref[k : k + 1, cols] += jnp.sum(pre_back * masked[k], axis=0, keepdims=True)
        cg_ref[KW : KW + 1, cols] += jnp.sum(pre_back, axis=0, keepdims=True)
        back = cw_ref[KW - 1 : KW, cols] * pre_back
        for k in range(KW - 1):
            z = pre_back * f["usable"][k]
            shifted_back[k, 0:span, cols] = z
            back = back + cw_ref[k : k + 1, cols] * shifted_back[k, KW - 1 - k : KW - 1 - k + span, cols]
            shifted_back[k, span : span + 8, cols] = z[0:8]
        out = c * LANES if c * LANES < ch else c * LANES + ch
        pb_ref[:, out : out + LANES] = back.astype(BF)


def scan_specs(rp, seqs, local, span, ch, backward):
    def block(s):
        return seqs - 1 - s if backward else s

    def tokens_of(width, at):
        return pl.BlockSpec((None, None, None, span, width), lambda q, s: (q // local, block(s), q % local, 0, at))

    def tail_of(width, at):
        return pl.BlockSpec(
            (None, None, None, 16, width),
            lambda q, s: (q // local, jnp.maximum(block(s) - 1, 0), q % local, span // 16 - 1, at),
        )

    def whole(*shape):
        return pl.BlockSpec(shape, lambda q, s: (0,) * len(shape))

    def rows_of(rows):
        return pl.BlockSpec((None, None, None, rows, span), lambda q, s: (q // local, block(s), q % local, 0, 0))

    def state_of():
        return pl.BlockSpec((None, None, None, N, ch), lambda q, s: (q // local, block(s), q % local, 0, 0))

    return tokens_of, tail_of, whole, rows_of, state_of


def constants(heads, ch, span):
    e = np.repeat(np.eye(heads, dtype=np.float32), PD, axis=1)
    i = np.eye(heads, LANES, dtype=np.float32)
    upper = np.triu(np.ones((span, span), np.float32))
    pick = np.zeros((8, 2 * LANES), np.float32)
    pick[0, :LANES] = 1.0
    pick[1, LANES:] = 1.0
    return tuple(jnp.asarray(v, BF) for v in (np.tile(e, (3, 1)), np.tile(i, (3, 1)), upper, upper.T, np.tile(pick, (3, 1))))


def front_specs(specs, ch, heads, span):
    tokens_of, tail_of, whole, rows_of, _ = specs
    wide = ch + 2 * N
    return [
        tokens_of(ch, 0), tail_of(ch, 0), tokens_of(2 * N, 2 * ch // (2 * N)), tail_of(2 * N, 2 * ch // (2 * N)),
        tokens_of(ch, 1), tokens_of(LANES, (2 * ch + 2 * N) // LANES), rows_of(1),
        whole(8, wide), whole(heads, LANES), whole(1, ch), whole(3 * heads, ch), whole(3 * heads, LANES), whole(span, span),
    ]


def mixer_forward(proj, doc, cw, hp, sk, consts):
    rp, seqs, local, span, _ = proj.shape
    heads, ch = hp.shape[0], sk.shape[1]
    wide = ch + 2 * N
    specs = scan_specs(rp, seqs, local, span, ch, False)
    tokens_of, tail_of, whole, rows_of, state_of = specs
    lead = (rp, seqs, local)
    e3, i3, upper, _, _ = consts
    return pl.pallas_call(
        forward_kernel,
        grid=(rp * local, seqs),
        in_specs=front_specs(specs, ch, heads, span),
        out_specs=[tokens_of(ch, 0), tokens_of(ch, 0), rows_of(8), state_of()],
        out_shape=[
            jax.ShapeDtypeStruct(lead + (span, ch), BF),
            jax.ShapeDtypeStruct(lead + (span, ch), BF),
            jax.ShapeDtypeStruct(lead + (8, span), F32),
            jax.ShapeDtypeStruct(lead + (N, ch), F32),
        ],
        scratch_shapes=[pltpu.VMEM((span + 16, wide), F32), pltpu.VMEM((span, wide), F32), pltpu.VMEM((N, ch), F32)],
        compiler_params=pltpu.CompilerParams(vmem_limit_bytes=40 * 2**20),
        cost_estimate=pl.CostEstimate(flops=20 * 10**9, bytes_accessed=30 * 10**6, transcendentals=0),
        name="mixer_forward",
    )(proj, proj, proj, proj, proj, proj, doc, cw, hp, sk, e3, i3, upper)


def mixer_backward(proj, doc, cw, hp, sk, consts, y, t1, stat, entry):
    rp, seqs, local, span, columns = proj.shape
    heads, ch = hp.shape[0], sk.shape[1]
    wide = ch + 2 * N
    specs = scan_specs(rp, seqs, local, span, ch, True)
    tokens_of, tail_of, whole, rows_of, state_of = specs
    lead = (rp, seqs, local)
    e3, i3, upper, lower, pick = consts
    return pl.pallas_call(
        backward_kernel,
        grid=(rp * local, seqs),
        in_specs=front_specs(specs, ch, heads, span)
        + [whole(span, span), whole(24, 2 * LANES), tokens_of(ch, 0), tokens_of(ch, 0), rows_of(8), state_of()],
        out_specs=[tokens_of(columns, 0), whole(8, wide), whole(2 * heads, span), whole(8, ch)],
        out_shape=[
            jax.ShapeDtypeStruct(lead + (span, columns), BF),
            jax.ShapeDtypeStruct((8, wide), F32),
            jax.ShapeDtypeStruct((2 * heads, span), F32),
            jax.ShapeDtypeStruct((8, ch), F32),
        ],
        scratch_shapes=[
            pltpu.VMEM((span + 16, wide), F32), pltpu.VMEM((span, wide), F32), pltpu.VMEM((span, wide), F32),
            pltpu.VMEM((KW - 1, span + 8, wide), F32), pltpu.VMEM((N, ch), F32), pltpu.VMEM((span, span), F32),
            pltpu.VMEM((8, span), F32),
        ],
        compiler_params=pltpu.CompilerParams(vmem_limit_bytes=48 * 2**20),
        cost_estimate=pl.CostEstimate(flops=60 * 10**9, bytes_accessed=60 * 10**6, transcendentals=0),
        name="mixer_backward",
    )(proj, proj, proj, proj, proj, proj, doc, cw, hp, sk, e3, i3, upper, lower, pick, y, t1, stat, entry)


def per_device(tokens, doc_start, cotangent, norm_gain, input_matrix, conv_weight, conv_bias, step_bias, decay_log, skip_gain,
               gate_gain, output_matrix):
    rp, seqs, fs, groups = (lax.axis_size(a) for a in ("rep", "seq", "fsdp", "group"))
    r, s, z = (lax.axis_index(a) for a in ("rep", "seq", "fsdp"))
    local, span, width = tokens.shape
    mine = local * span
    tp = rp * seqs
    heads = H // tp
    ch = heads * PD
    cc = DI + 2 * N
    part = s * rp + r
    plane = ("rep", "seq")
    rows = input_matrix.shape[0]
    out_rows = output_matrix.shape[0]
    conv_rows = conv_weight.shape[0]
    head_rows = step_bias.shape[0]

    doc_f = doc_start.astype(F32).reshape(-1)
    small = [conv_weight.astype(F32).reshape(-1), conv_bias.astype(F32), step_bias.astype(F32), decay_log.astype(F32),
             skip_gain.astype(F32), doc_f]
    small = jnp.concatenate(small)
    small = jnp.pad(small, (0, -small.shape[0] % 1024)).reshape(1, 1, 1, -1)
    everything = lax.all_gather(small, ("rep", "seq", "fsdp"), axis=0, tiled=True).reshape(rp, seqs, fs, -1)
    at = 0

    def taken(count):
        nonlocal at
        at += count
        return everything[0, :, :, at - count : at].reshape(-1)

    conv_w = taken(conv_rows * KW).reshape(cc, KW)
    conv_b = taken(conv_rows)
    bias_all, log_all, skip_all = taken(head_rows), taken(head_rows), taken(head_rows)
    doc = lax.dynamic_index_in_dim(everything[..., at : at + mine], z, axis=2, keepdims=False)
    doc = doc.reshape(rp, seqs, local, 1, span)
    table = jnp.concatenate([conv_w.T, conv_b[None], jnp.zeros((8 - KW - 1, cc), F32)], axis=0)
    cw = jnp.concatenate([lax.dynamic_slice_in_dim(table, part * ch, ch, axis=1), table[:, DI:]], axis=1)
    hp = jnp.stack([bias_all, log_all], axis=1)
    hp = jnp.pad(lax.dynamic_slice_in_dim(hp, part * heads, heads, axis=0), ((0, 0), (0, LANES - 2)))
    sk = jnp.repeat(lax.dynamic_slice_in_dim(skip_all, part * heads, heads, axis=0), PD)[None]
    consts = constants(heads, ch, span)

    wide_tokens = tokens.astype(F32).reshape(mine, width)
    inv_in = lax.rsqrt(jnp.mean(wide_tokens * wide_tokens, axis=-1, keepdims=True) + EPSILON)
    unit = wide_tokens * inv_in
    u = unit.astype(BF).reshape(mine, seqs, fs, rows).swapaxes(1, 2).reshape(mine, width)
    all_u = lax.all_gather(u, plane, axis=0, tiled=True)

    gain = norm_gain.astype(F32)[:, None]
    scaled = (input_matrix.astype(F32) * gain).astype(BF)

    def columns_of(values, each):
        split = values.reshape(rows, seqs, rp, each)
        return lax.dynamic_index_in_dim(split, r, axis=2, keepdims=False)

    pieces = [
        columns_of(scaled[:, DI : 2 * DI], ch), columns_of(scaled[:, :DI], ch),
        jnp.broadcast_to(scaled[:, None, 2 * DI : 2 * DI + 2 * N], (rows, seqs, 2 * N)),
        columns_of(scaled[:, 2 * DI + 2 * N :], heads), jnp.zeros((rows, seqs, LANES - heads), BF),
    ]
    sent = jnp.concatenate(pieces, axis=-1).swapaxes(0, 1)
    columns = sent.shape[-1]
    w_in = lax.all_to_all(sent, "seq", 0, 0, tiled=True)
    w_in = lax.all_gather(w_in, "fsdp", axis=0, tiled=True).reshape(width, columns)

    gate = gate_gain.astype(F32)[:, None]
    scaled_out = (output_matrix.astype(F32) * gate).astype(BF)
    w_out = lax.all_gather(scaled_out, "fsdp", axis=0, tiled=True)
    w_out = lax.dynamic_slice_in_dim(w_out, r * ch, ch, axis=0)
    all_cot = lax.all_gather(cotangent.reshape(mine, width), plane, axis=0, tiled=True)

    proj = nn(all_u, w_in).astype(BF).reshape(rp, seqs, local, span, columns)
    y, gated, s1, entry = mixer_forward(proj, doc, cw, hp, sk, consts)
    count = tp * mine
    gated = gated.reshape(count, ch)
    t1 = nt(all_cot, w_out)
    s2 = jnp.sum(t1 * gated.astype(F32), axis=-1).reshape(rp, seqs, local, span)
    stats = lax.psum(jnp.stack([s1[..., 0, :], s2]), plane)
    inv = lax.rsqrt(stats[0] * (1.0 / DI) + EPSILON)
    kk = inv * inv * inv * stats[1] * (1.0 / DI)
    stat = jnp.pad(jnp.stack([inv, kk], axis=3), ((0, 0),) * 3 + ((0, 6), (0, 0)))

    branch = lax.psum_scatter(nn(gated, w_out).astype(BF), plane, scatter_dimension=0, tiled=True)
    own_inv = lax.dynamic_slice(inv, (r, s, 0, 0), (1, 1, local, span)).reshape(mine, 1)
    layer_out = (wide_tokens + branch.astype(F32) * own_inv).astype(BF).reshape(tokens.shape)

    mixed = (gated.astype(F32) * inv.reshape(count, 1)).astype(BF)
    out_part = tn(mixed, all_cot).astype(BF)

    pb, cg, hg, sg = mixer_backward(proj, doc, cw, hp, sk, consts, y, t1.astype(BF).reshape(y.shape), stat, entry)
    pb = pb.reshape(count, columns)
    back = lax.psum_scatter(nt(pb, w_in).astype(BF), plane, scatter_dimension=0, tiled=True)
    in_part = tn(all_u, pb).astype(BF)

    piece = ch // fs
    out_sum = lax.psum_scatter(out_part, "fsdp", scatter_dimension=0, tiled=True)
    out_sum = lax.all_gather(out_sum, plane[0], axis=0, tiled=False) if False else out_sum
    out_all = lax.all_gather(out_sum, ("rep", "fsdp"), axis=0, tiled=True)
    out_own = lax.dynamic_slice_in_dim(out_all, z * out_rows, out_rows, axis=0).astype(F32)

    in_sum = lax.psum_scatter(in_part, "fsdp", scatter_dimension=0, tiled=True)
    in_sum = lax.all_to_all(in_sum.reshape(seqs, rows, columns), "seq", 0, 0, tiled=True)
    shared = jnp.sum(in_sum[:, :, 2 * ch : 2 * ch + 2 * N].astype(F32), axis=0)
    in_both = lax.all_gather(in_sum, "rep", axis=0)
    shared = lax.psum(shared, "rep")
    in_both = in_both.transpose(2, 1, 0, 3)

    def back_columns(begin, each):
        return in_both[..., begin : begin + each].reshape(rows, tp * each).astype(F32)

    in_own = jnp.concatenate([back_columns(ch, ch), back_columns(0, ch), shared, back_columns(2 * ch + 2 * N, heads)], axis=1)

    conv_grad = jnp.zeros((KW + 1, cc), F32)
    conv_grad = lax.dynamic_update_slice_in_dim(conv_grad, cg[: KW + 1, :ch], part * ch, axis=1)
    conv_grad = lax.dynamic_update_slice_in_dim(conv_grad, cg[: KW + 1, ch:], DI, axis=1)
    by_head = jnp.stack([jnp.sum(hg[:heads], axis=1), jnp.sum(hg[heads:], axis=1), jnp.sum(sg[0].reshape(heads, PD), axis=1)])
    head_grad = lax.dynamic_update_slice_in_dim(jnp.zeros((3, H), F32), by_head, part * heads, axis=1)
    packed = jnp.concatenate([conv_grad.reshape(-1), head_grad.reshape(-1)])
    size = packed.shape[0]
    packed = jnp.pad(packed, (0, -size % 1024)).reshape(-1, LANES)
    packed = lax.psum(packed, ("group", "rep", "seq", "fsdp")).reshape(-1)
    conv_grad = packed[: (KW + 1) * cc].reshape(KW + 1, cc)
    head_grad = packed[(KW + 1) * cc : size].reshape(3, H)
    owner = s * fs + z
    conv_own = lax.dynamic_slice_in_dim(conv_grad, owner * conv_rows, conv_rows, axis=1)
    head_own = lax.dynamic_slice_in_dim(head_grad, owner * head_rows, head_rows, axis=1)

    if groups > 1:
        out_own, in_own = lax.psum((out_own, in_own), "group")
    weight = input_matrix.astype(F32)
    norm_gain_grad = jnp.sum(weight * in_own, axis=1)
    in_own = in_own * gain
    gate_gain_grad = jnp.sum(output_matrix.astype(F32) * out_own, axis=1)
    out_own = out_own * gate

    v = back.astype(F32).reshape(mine, fs, seqs, rows).swapaxes(1, 2).reshape(mine, width)
    tokens_grad = cotangent.astype(F32).reshape(mine, width) + inv_in * (v - unit * jnp.mean(v * unit, axis=-1, keepdims=True))

    return (
        layer_out, tokens_grad.reshape(tokens.shape), norm_gain_grad, in_own, conv_own[:KW].T, conv_own[KW], head_own[0], head_own[1],
        head_own[2], gate_gain_grad, out_own,
    )


def solution(mesh):
    rep, seqs, fs = (mesh.shape[a] for a in ("rep", "seq", "fsdp"))
    pair = 2 if rep % 2 == 0 else 1
    devices = np.asarray(mesh.devices).reshape(rep // pair, pair, seqs, fs)
    planes = Mesh(devices, ("group", "rep", "seq", "fsdp"))
    batch = ("group", "rep", "fsdp")
    by_token = P(batch, "seq", None)
    vector = P(("seq", "fsdp"))
    matrix = P(("seq", "fsdp"), None)
    return jax.shard_map(
        per_device,
        mesh=planes,
        in_specs=(by_token, P(batch, "seq"), by_token, vector, matrix, matrix, vector, vector, vector, vector, vector, matrix),
        out_specs=(by_token, by_token, vector, matrix, matrix, vector, vector, vector, vector, vector, matrix),
        check_vma=False,
    )
```

time: 1890 us -> 1220 us (0.65)
  matrix products: 414 us -> 142 us
  waiting for transfers between devices: 867 us -> 681 us
  other arithmetic: 184 us -> 44.3 us
  Pallas kernels: 0 us -> 117 us
  blocking collectives: 239 us -> 146 us
  local copies, waits for them, and re-layouts: 146 us -> 69.6 us
    reduce_scatter x2 -> x4, waiting for transfers between devices: 676 us -> 292 us  [the longest x1 107 us: per_device(): lax.psum_scatter(nt(pb, w_in).astype(BF), plane, scatter_dimension=0, til...]
    dot_general x36 -> x6, matrix products: 414 us -> 142 us  [dot(): return lax.dot_general(a, b, (dims, ((), ())), preferred_element_type=F32)]
    all_gather x6, waiting for transfers between devices: 78.7 us -> 314 us  [the longest x1 90.9 us: per_device(): all_u = lax.all_gather(u, plane, axis=0, tiled=True)]
    unnamed x2 -> x0, blocking collectives: 122 us -> none
    pallas_call x0 -> x2, Pallas kernels: none -> 117 us  [the longest x1 79.9 us: mixer_backward(): pl.pallas_call(backward_kernel, grid=(rp * local, seqs), in_specs=front_s...]
    reduce_sum x16 -> x5, other arithmetic: 73.7 us -> 11.7 us  [the longest x1 10.2 us: per_device(): jnp.mean(v * unit, axis=-1, keepdims=True)]
    all_to_all x0 -> x2, blocking collectives: none -> 45.2 us  [the longest x1 22.8 us: per_device(): w_in = lax.all_to_all(sent, 'seq', 0, 0, tiled=True)]
    mul x24 -> x0, local copies, waits for them, and re-layouts: 39.3 us -> none  [the longest x8 27.9 us: carried_mix(): jnp.einsum('stn,shpn->sthp', read_vec, state_in, precision=EXACT_MATMUL)]
  transfers between devices with their start and end apart: 14 -> 12, of which waited for: 7 -> 11; matrix products, arithmetic and copies ran while one was open for 35% -> 16% of each run, Pallas kernels for 0% -> 10%
where the time goes in v1:
time: 1220 us
  waiting for transfers between devices  681 us (56%)
  blocking collectives  146 us (12%)
  matrix products  142 us (12%)
  Pallas kernels  117 us (10%)
  local copies, waits for them, and re-layouts  69.6 us (6%)
  other arithmetic  44.3 us (4%)
  between operations  15 us (1%)
    dot_general x6, matrix products, dot(): return lax.dot_general(a, b, (dims, ((), ())), preferred_element_type=F32)  142 us
    reduce_scatter x1, waiting for transfers between devices, per_device(): lax.psum_scatter(nt(pb, w_in).astype(BF), plane, scatter_dimension=0, til...  107 us
    reduce_scatter x1, waiting for transfers between devices, per_device(): in_sum = lax.psum_scatter(in_part, 'fsdp', scatter_dimension=0, tiled=True)  100 us
    all_gather x1, waiting for transfers between devices, per_device(): all_u = lax.all_gather(u, plane, axis=0, tiled=True)  90.9 us
    all_gather x1, waiting for transfers between devices, per_device(): lax.all_gather(cotangent.reshape(mine, width), plane, axis=0, tiled=True)  90.2 us
    reduce_scatter x1, waiting for transfers between devices, per_device(): lax.psum_scatter(nn(gated, w_out).astype(BF), plane, scatter_dimension=0,...  84.6 us
    pallas_call x1, Pallas kernels, mixer_backward(): pl.pallas_call(backward_kernel, grid=(rp * local, seqs), in_specs=front_s...  79.9 us
    all_gather x1, blocking collectives, per_device(): lax.all_gather(small, ('rep', 'seq', 'fsdp'), axis=0, tiled=True)  76.5 us
  transfers between devices with their start and end apart: 12, of which 11 were waited for; matrix products, arithmetic and copies ran while one was open for 16% of the time, Pallas kernels for 10%

profile of v1, /device:TPU:0, one launch (start us, length us, event | category | flops | bytes accessed | tf_op | source)
XLA Modules:
  0.0 1215.9 jit_solution(4502441707041165398)
XLA Ops:
  7.9 1.8 fusion.2
  10.0 1.0 copy.89
  11.9 1.0 copy.88
  14.3 2.6 concatenate.18
  16.9 22.8 %all_to_all.10 = bf16[4,128,1408]{2,1,0:T(8,128)(2,1)} all-to-all(bf16[4,128,1408]{2,1,0:T(8,128)(2,1)S(1)} %bitcast.90), channel_id=1, replica_groups=mesh['rep'=2,'seq'=4,'fsdp'=4] {'seq'}, dimensions={0} | all-to-all | bytes 2883584 | tf_op jit(solution)/shard_map/all_to_all | solution.py:463
  39.8 4.5 reshape.241
  45.9 5.8 fusion.15
  51.7 2.8 reshape.242
  55.2 1.2 fusion.13
  57.5 76.5 %all-gather = f32[65536]{0:T(1024)S(1)} all-gather(f32[2048]{0:T(1024)S(1)} %pad.16), channel_id=2, replica_groups=mesh['rep'=2,'seq'=4,'fsdp'=4] {'rep','seq','fsdp'}, dimensions={0}, use_global_device_ids=true | all-gather | bytes 270336 | tf_op jit(solution)/shard_map/all_gather | solution.py:423
  135.2 1.2 reshape_reshape_squeeze.3
  137.3 15.2 %all-gather.11.cloned.1.call-done = bf16[16,128,1408]{2,1,0:T(8,128)(2,1)} async-done(((bf16[4,128,1408]{2,1,0:T(8,128)(2,1)}), bf16[16,128,1408]{2,1,0:T(8,128)(2,1)}) %all-gather.11.cloned.1.call-update) | async-done | bytes 5767184 | tf_op jit(solution)/shard_map/all_gather | solution.py:464
  152.5 90.9 %all-gather.9.cloned.1.call-done = bf16[4096,2048]{1,0:T(8,128)(2,1)} async-done(((bf16[512,2048]{1,0:T(8,128)(2,1)}), bf16[4096,2048]{1,0:T(8,128)(2,1)}) %all-gather.9.cloned.1.call-update) | async-done | bytes 16777232 | tf_op jit(solution)/shard_map/all_gather | solution.py:447
  243.4 32.1 %convolution_convert_fusion.2 = bf16[4096,1408]{1,0:T(8,128)(2,1)} fusion(bf16[4096,2048]{1,0:T(8,128)(2,1)} %all-gather.9.cloned.1.call-done, bf16[2048,1408]{1,0:T(8,128)(2,1)} %bitcast.114), kind=kOutput, calls=%fused_computation.2 | convolution fusion | flops 23628087296 | bytes 34078720 | tf_op jit(solution)/shard_map/dot_general | solution.py:24
  275.5 37.1 %mixer_forward.1 = (bf16[2,4,2,256,512]{4,3,2,1,0:T(8,128)(2,1)S(1)}, bf16[2,4,2,256,512]{4,3,2,1,0:T(8,128)(2,1)S(1)}, f32[2,4,2,8,256]{4,3,2,1,0:T(8,128)S(1)}, f32[2,4,2,128,512]{4,3,2,1,0:T(8,128)S(1)}) custom-call(bf16[2,4,2,256,1408]{4,3,2,1,0:T(8,128)(2,1)} %bitcast.118, bf16[2,4,2,256,1408]{4,3,2,1,0:T(8,128)(2,1)} %bitcast.119, ...), custom_call_target="tpu_custom_call" | custom-call | flops 20000000000 | bytes 30000000 | tf_op jit(solution)/shard_map/mixer_forward/pallas_call | solution.py:352
  312.6 2.0 copy-done
  314.7 2.1 copy-done.6
  316.7 2.0 copy-done.8
  318.7 6.4 copy.83
  325.1 1.2 all-gather.13.cloned.1.call-done
  326.3 90.2 %all-gather.15.cloned.1.call-done = bf16[4096,2048]{1,0:T(8,128)(2,1)} async-done(((bf16[512,2048]{1,0:T(8,128)(2,1)}), bf16[4096,2048]{1,0:T(8,128)(2,1)}) %all-gather.15.cloned.1.call-update) | async-done | bytes 16777232 | tf_op jit(solution)/shard_map/all_gather | solution.py:470
  416.5 15.0 %fusion = (f32[4096]{0:T(1024)S(1)}, bf16[512,4096]{1,0:T(8,128)(2,1)}) fusion(bf16[4096,512]{0,1:T(8,128)(2,1)} %copy.83, bf16[4096,2048]{1,0:T(8,128)(2,1)} %all-gather.15.cloned.1.call-done, bf16[1024,2048]{1,0:T(8,128)(2,1)} %all-gather.13.cloned.1.call-done, s32[]{:T(128)S(6)} %select_n.40), kind=kOutput, calls=%fused_computation.5 | convolution fusion | flops 8598319104 | bytes 27279364 | tf_op jit(solution)/shard_map/dot_general | solution.py:24
  431.5 24.0 %psum.21 = f32[2,2,4,2,256]{4,0,3,2,1:T(2,128)S(1)} all-reduce(f32[2,2,4,2,256]{4,0,3,2,1:T(2,128)S(1)} %pad_maximum_fusion.1), channel_id=1, replica_groups=mesh['rep'=2,'seq'=4,'fsdp'=4] {'rep','seq'}, use_global_device_ids=true, to_apply=%region_3.4 | all-reduce | flops 8192 | bytes 65536 | tf_op jit(solution)/shard_map/psum | solution.py:478
  455.5 6.5 copy.84
  462.1 14.6 %fusion.9 = bf16[512,2048]{1,0:T(8,128)(2,1)} fusion(bf16[4096,2048]{1,0:T(8,128)(2,1)} %all-gather.15.cloned.1.call-done, bf16[4096,512]{0,1:T(8,128)(2,1)} %copy.83, f32[4096]{0:T(1024)S(1)} %bitcast.103), kind=kOutput, calls=%fused_computation.23 | convolution fusion | flops 8597274624 | bytes 23085056 | tf_op jit(solution)/shard_map/dot_general | solution.py:24
  476.8 2.2 copy-done.7
  479.0 79.9 %mixer_backward.1 = (bf16[2,4,2,256,1408]{4,3,2,1,0:T(8,128)(2,1)}, f32[8,768]{1,0:T(8,128)S(1)}, f32[16,256]{1,0:T(8,128)S(1)}, f32[8,512]{1,0:T(8,128)S(1)}) custom-call(bf16[2,4,2,256,1408]{4,3,2,1,0:T(8,128)(2,1)} %bitcast.124, bf16[2,4,2,256,1408]{4,3,2,1,0:T(8,128)(2,1)} %bitcast.125, bf16[2,4,2,256,1408]{4,3,2,1,0:T(8,128)(2,1)} %bitcast.126, ...), custom_call_target="tpu_custom_call" | custom-call | flops 60000002048 | bytes 60000000 | tf_op jit(solution)/shard_map/mixer_backward/pallas_call | solution.py:378
  558.9 33.6 %convolution_convert_fusion.3 = bf16[2048,1408]{1,0:T(8,128)(2,1)} fusion(bf16[4096,2048]{1,0:T(8,128)(2,1)} %all-gather.9.cloned.1.call-done, bf16[4096,1408]{1,0:T(8,128)(2,1)} %bitcast.116), kind=kOutput, calls=%fused_computation.8 | convolution fusion | flops 23625203712 | bytes 34078720 | tf_op jit(solution)/shard_map/dot_general | solution.py:24
  594.8 100.2 %reduce-scatter.9.cloned.1.call-done = bf16[512,1408]{1,0:T(8,128)(2,1)} async-done(((bf16[2048,1408]{1,0:T(8,128)(2,1)}), bf16[512,1408]{1,0:T(8,128)(2,1)}) %reduce-scatter.9.cloned.1.call-update) | async-done | bytes 1441808 | tf_op jit(solution)/shard_map/reduce_scatter | solution.py:501
  695.0 22.4 %all_to_all.11 = bf16[4,128,1408]{2,1,0:T(8,128)(2,1)S(1)} all-to-all(bf16[4,128,1408]{2,1,0:T(8,128)(2,1)} %bitcast.99), channel_id=1, replica_groups=mesh['rep'=2,'seq'=4,'fsdp'=4] {'seq'}, dimensions={0} | all-to-all | bytes 2883584 | tf_op jit(solution)/shard_map/all_to_all | solution.py:502
  719.0 32.3 %convolution_convert_fusion = bf16[4096,2048]{1,0:T(8,128)(2,1)} fusion(bf16[4096,1408]{1,0:T(8,128)(2,1)} %bitcast.117, bf16[2048,1408]{1,0:T(8,128)(2,1)} %bitcast.115), kind=kOutput, calls=%fused_computation | convolution fusion | flops 23630708736 | bytes 34078720 | tf_op jit(solution)/shard_map/dot_general | solution.py:24
  751.4 14.9 %convolution_convert_fusion.1 = bf16[4096,2048]{1,0:T(8,128)(2,1)} fusion(bf16[4096,512]{1,0:T(8,128)(2,1)} %bitcast.83, bf16[1024,2048]{1,0:T(8,128)(2,1)} %all-gather.13.cloned.1.call-done, s32[]{:T(128)S(6)} %select_n.40), kind=kOutput, calls=%fused_computation.1 | convolution fusion | flops 8598323200 | bytes 23068676 | tf_op jit(solution)/shard_map/dot_general | solution.py:24
  767.0 55.2 %all-reduce.9.cloned.1.call-done = f32[176,128]{1,0:T(8,128)} async-done(((f32[176,128]{1,0:T(8,128)}), f32[176,128]{1,0:T(8,128)}) %all-reduce.9.cloned.1.call-update) | async-done | bytes 90128 | tf_op jit(solution)/shard_map/psum | solution.py:521
  826.1 73.3 %all-gather.17.cloned.1.call-done = bf16[1024,2048]{1,0:T(8,128)(2,1)} async-done(((bf16[128,2048]{1,0:T(8,128)(2,1)}), bf16[1024,2048]{1,0:T(8,128)(2,1)}) %all-gather.17.cloned.1.call-update) | async-done | bytes 4194320 | tf_op jit(solution)/shard_map/all_gather | solution.py:498
  899.4 3.6 convert_multiply_fusion.4
  902.9 18.5 %all-reduce.7.cloned.1.call-done = f32[128,256]{1,0:T(8,128)} async-done(((f32[128,256]{1,0:T(8,128)}), f32[128,256]{1,0:T(8,128)}) %all-reduce.7.cloned.1.call-update) | async-done | bytes 131088 | tf_op jit(solution)/shard_map/psum | solution.py:505
  922.4 43.1 %all-gather.19.cloned.1.call-done = bf16[8,128,1408]{2,1,0:T(8,128)(2,1)} async-done(((bf16[4,128,1408]{2,1,0:T(8,128)(2,1)}), bf16[8,128,1408]{2,1,0:T(8,128)(2,1)}) %all-gather.19.cloned.1.call-update) | async-done | bytes 2883600 | tf_op jit(solution)/shard_map/all_gather | solution.py:504
  965.5 3.4 copy.86
  969.5 1.2 copy-done.11
  970.7 7.7 fusion.12
  978.4 107.1 %reduce-scatter.7.cloned.1.call-done = bf16[512,2048]{1,0:T(8,128)(2,1)} async-done(((bf16[4096,2048]{1,0:T(8,128)(2,1)}), bf16[512,2048]{1,0:T(8,128)(2,1)}) %reduce-scatter.7.cloned.1.call-update) | async-done | bytes 2097168 | tf_op jit(solution)/shard_map/reduce_scatter | solution.py:492
  1085.5 6.1 reshape.271
  1091.5 10.2 multiply_reduce_fusion
  1101.7 6.4 copy.85
  1108.1 6.1 reshape.260
  1114.2 6.4 multiply_add_fusion
  1120.6 84.6 %reduce-scatter.5.cloned.1.call-done = bf16[512,2048]{1,0:T(8,128)(2,1)} async-done(((bf16[4096,2048]{1,0:T(8,128)(2,1)}), bf16[512,2048]{1,0:T(8,128)(2,1)}) %reduce-scatter.5.cloned.1.call-update) | async-done | bytes 2097168 | tf_op jit(solution)/shard_map/reduce_scatter | solution.py:483
  1205.3 3.6 fusion.6
  (158 shorter events, 18.7 us)
Async XLA Ops:
  7.2 145.3 %all-gather.11.cloned.1.call-start = ((), (), s32[]{:S(2)}) async-start(), calls=%async_computation.7 | async-start | bytes 7208960 | tf_op jit(solution)/shard_map/all_gather | solution.py:464
  7.9 1.8 copy-start.22
  11.9 27.9 %copy-start.9 = (bf16[2,256,2048]{2,1,0:T(8,128)(2,1)S(1)}, bf16[2,256,2048]{2,1,0:T(8,128)(2,1)}, u32[]{:S(2)}) copy-start(bf16[2,256,2048]{2,1,0:T(8,128)(2,1)} %param.17) | copy-start | bytes 6291460
  39.7 203.7 %all-gather.9.cloned.1.call-start = ((), (), s32[]{:S(2)}) async-start(), calls=%async_computation.6 | async-start | bytes 18874368 | tf_op jit(solution)/shard_map/all_gather | solution.py:447
  45.4 0.5 copy-start.16
  51.7 2.9 copy-start.29
  51.7 3.5 copy-start.13
  54.5 2.6 copy-start.24
  54.5 2.6 copy-start.21
  54.5 2.9 copy-start.25
  54.5 2.9 copy-start.26
  54.5 2.9 copy-start.27
  54.6 2.9 copy-start.28
  54.6 271.7 %all-gather.13.cloned.1.call-start = ((), (), s32[]{:S(2)}) async-start(), calls=%async_computation.8 | async-start | bytes 5242880 | tf_op jit(solution)/shard_map/all_gather | solution.py:468
  54.7 0.6 copy-start.19
  56.5 360.0 %all-gather.15.cloned.1.call-start = ((), (), s32[]{:S(2)}) async-start(), calls=%async_computation.10 | async-start | bytes 18874368 | tf_op jit(solution)/shard_map/all_gather | solution.py:470
  57.0 537.1 %reduce-scatter.11.cloned.1.call-start = ((), (), s32[]{:S(2)}) async-start(), calls=%async_computation.15 | async-start | bytes 2621440 | tf_op jit(solution)/shard_map/reduce_scatter | solution.py:496
  243.4 32.1 %copy-start.1 = (bf16[256,256]{1,0:T(8,128)(2,1)S(1)}, bf16[256,256]{1,0:T(8,128)(2,1)}, u32[]{:S(2)}) copy-start(bf16[256,256]{1,0:T(8,128)(2,1)} %constant.79.clone.tri_ref) | copy-start | bytes 393220
  243.4 32.1 %copy-start.3 = (bf16[24,512]{1,0:T(8,128)(2,1)S(1)}, bf16[24,512]{1,0:T(8,128)(2,1)}, u32[]{:S(2)}) copy-start(bf16[24,512]{1,0:T(8,128)(2,1)} %constant.77.clone.e3_ref) | copy-start | bytes 73732
  243.4 32.1 %copy-start.5 = (bf16[24,128]{1,0:T(8,128)(2,1)S(1)}, bf16[24,128]{1,0:T(8,128)(2,1)}, u32[]{:S(2)}) copy-start(bf16[24,128]{1,0:T(8,128)(2,1)} %constant.78.clone.i3_ref) | copy-start | bytes 18436
  312.6 2.0 copy-start
  314.7 2.1 copy-start.6
  316.7 2.0 copy-start.8
  462.1 14.7 %copy-start.15 = (f32[1,2,4,2,256]{4,0,3,2,1:T(1,128)}, f32[1,2,4,2,256]{4,0,3,2,1:T(1,128)S(1)}, u32[]{:S(2)}) copy-start(f32[1,2,4,2,256]{4,0,3,2,1:T(1,128)S(1)} %get-tuple-element.30) | copy-start | bytes 49156
  462.1 14.8 %copy-start.2 = (bf16[256,256]{1,0:T(8,128)(2,1)S(1)}, bf16[256,256]{1,0:T(8,128)(2,1)}, u32[]{:S(2)}) copy-start(bf16[256,256]{1,0:T(8,128)(2,1)} %constant.80.clone.low_ref) | copy-start | bytes 393220
  462.1 14.7 %copy-start.4 = (bf16[24,256]{1,0:T(8,128)(2,1)S(1)}, bf16[24,256]{1,0:T(8,128)(2,1)}, u32[]{:S(2)}) copy-start(bf16[24,256]{1,0:T(8,128)(2,1)} %constant.81.clone.pick_ref) | copy-start | bytes 36868
  476.7 218.3 %reduce-scatter.9.cloned.1.call-start = ((), (), s32[]{:S(2)}) async-start(), calls=%async_computation.12 | async-start | bytes 7208960 | tf_op jit(solution)/shard_map/reduce_scatter | solution.py:501
  476.8 2.2 copy-start.7
  592.6 229.6 %all-reduce.9.cloned.1.call-start = ((), (), s32[]{:S(2)}) async-start(), calls=%async_computation.14 | async-start | bytes 180224 | tf_op jit(solution)/shard_map/psum | solution.py:521
  594.0 305.3 %all-gather.17.cloned.1.call-start = ((), (), s32[]{:S(2)}) async-start(), calls=%async_computation.16 | async-start | bytes 4718592 | tf_op jit(solution)/shard_map/all_gather | solution.py:498
  594.8 326.6 %all-reduce.7.cloned.1.call-start = ((), (), s32[]{:S(2)}) async-start(), calls=%async_computation.13 | async-start | bytes 262144 | tf_op jit(solution)/shard_map/psum | solution.py:505
  717.4 1.1 copy-start.12
  718.2 247.3 %all-gather.19.cloned.1.call-start = ((), (), s32[]{:S(2)}) async-start(), calls=%async_computation.17 | async-start | bytes 4325376 | tf_op jit(solution)/shard_map/all_gather | solution.py:504
  718.8 366.7 %reduce-scatter.7.cloned.1.call-start = ((), (), s32[]{:S(2)}) async-start(), calls=%async_computation.11 | async-start | bytes 18874368 | tf_op jit(solution)/shard_map/reduce_scatter | solution.py:492
  751.3 454.0 %reduce-scatter.5.cloned.1.call-start = ((), (), s32[]{:S(2)}) async-start(), calls=%async_computation.9 | async-start | bytes 18874368 | tf_op jit(solution)/shard_map/reduce_scatter | solution.py:483
  766.2 133.1 %copy-start.14 = (bf16[256,2048]{1,0:T(8,128)(2,1)S(1)}, bf16[256,2048]{1,0:T(8,128)(2,1)}, u32[]{:S(2)}) copy-start(bf16[256,2048]{1,0:T(8,128)(2,1)} %param.28) | copy-start | bytes 3145732
  766.2 133.1 %copy-start.20 = (f32[256]{0:T(256)S(1)}, f32[256]{0:T(256)}, u32[]{:S(2)}) copy-start(f32[256]{0:T(256)} %copy-done.19) | copy-start | bytes 3076
  969.0 1.6 copy-start.11
  969.1 1.6 copy-start.23
  978.4 113.2 %copy-start.17 = (f32[1,2,2,128]{3,1,2,0:T(2,128)S(1)}, f32[1,2,2,128]{3,1,2,0:T(2,128)}, u32[]{:S(2)}) copy-start(f32[1,2,2,128]{3,1,2,0:T(2,128)} %copy-done.16) | copy-start | bytes 6148
  1108.1 6.1 copy-start.10
  1108.1 6.1 copy-start.18
Sparse Core Ops, SparseCore 0:
  39.8 112.6 all-gather.10
  155.0 88.3 all-gather.8
  245.5 80.7 all-gather.12
  328.1 88.3 all-gather.14
  476.8 43.8 reduce-scatter.10
  592.7 102.2 reduce-scatter.8
  701.5 120.6 all-reduce.8
  824.6 74.7 all-gather.16
  901.7 19.6 all-reduce.6
  923.5 41.9 all-gather.18
  969.5 115.9 reduce-scatter.6
  1089.3 115.9 reduce-scatter.4
